TPU v7x, 32 devices: a whole 2x2x4 slice. The times are simulated.
32 devices in a mesh: row: 4 (over z), col: 8 (over y, x, core).
Axes of the slice: x: 2, y: 2, z: 4, core: 2. Of those that a mesh axis runs over, the one named last changes fastest.
Arguments:
- config: float32 [6, 4096], P(None, ('row', 'col')), as said below
- start: float32 [6, 4096], P(None, ('row', 'col')), may hold values from -6 to 6
- tile_list: int32 [4, 8, 8, 5], P('row', 'col'), may hold values from -1 to 7, as said below
- tile_count: int32 [4, 8], P('row', 'col'), may hold values from 1 to 8, as said below
Outputs:
- coefficients: float32 [4], replicated
- mode: float32 [6, 4096], P(None, ('row', 'col'))
Inputs may be any that keep to these rules, and one draw needn't show every extreme that they name: `tile_list`: entry k of device (r, c) is used when k < tile_count[r, c]; its first value is a row tile 0 to 7, its second a column tile 0 to 3, the last three are offsets in -1, 0, 1, not all zero. Unused entries hold values of the same law. `tile_count`: some device uses all 8 entries. `config`: rows 3 to 5 are unit vectors. No two ellipsoids intersect, within a tile or across tiles placed by a list entry's offsets.
All inputs are finite; a program needn't handle non-finite values.
Results may differ from a plain program's by a relative error of at most 0.0003.
Values sent between devices are 32-bit elements; how exact they have to be, the bound alone decides.
No kernel may reach another device: no remote copies, remote signals or barrier semaphores. Data moves between devices by JAX's collectives and lax.ppermute only.
A program may use at most 64 MiB of HBM per device.

v0:
```python
import functools
import math

import jax
import jax.numpy as jnp
from jax import lax
from jax.experimental import pallas as pl
from jax.experimental.pallas import tpu as pltpu
from jax.sharding import PartitionSpec as P

chi_shape = 0.8
chi_energy = (math.sqrt(5.0) - 1.0) / (math.sqrt(5.0) + 1.0)
well_depth = 0.005
cutoff_sq = 20.25
norm_eps = 1e-06

SUB = 8
CENTRE = 6
LIST_ROW = 12
CODE_BITS = 6
ITEM_BITS = 8
ITEM_MASK = 255
LAYER = 16
TESTS = 5
GROUP = 4
TERMS = 20
HELD = 128
VMEM_LIMIT = 32 * 1024 * 1024
PACK_LIMIT = 60 * 1024 * 1024


def dot3(a, b):
    return a[0] * b[0] + a[1] * b[1] + a[2] * b[2]


def cross3(a, b):
    return (
        a[1] * b[2] - a[2] * b[1],
        a[2] * b[0] - a[0] * b[2],
        a[0] * b[1] - a[1] * b[0],
    )


def inverse(value):
    guess = pl.reciprocal(value, approx=True)
    return guess * (2.0 - value * guess)


def bracket(chi, scaled, factor, p, a, b):
    f = factor * (a - scaled * b)
    g = factor * (b - scaled * a)
    y = p * (a * f + b * g)
    cross = factor * scaled
    f_c = chi * (cross * f - factor * g)
    g_c = chi * (cross * g - factor * f)
    return f, g, y, cross, f_c, g_c


def pair_coefficients(d, ui, uj, lift):
    r_sq = dot3(d, d) + lift
    a = dot3(d, ui)
    b = dot3(d, uj)
    c = dot3(ui, uj)
    r_inv = lax.rsqrt(r_sq)
    p = r_inv * r_inv
    p2 = 2.0 * p
    r = r_sq * r_inv
    x = jnp.maximum(1.0 - r_sq * (1.0 / cutoff_sq), 0.0)
    c_shape = chi_shape * c
    c_energy = chi_energy * c
    e1 = lax.rsqrt(1.0 - c_shape * c_shape)
    q = e1 * e1
    q2 = inverse(1.0 - c_energy * c_energy)
    f, g, y, m, f_c, g_c = bracket(chi_shape, c_shape, q, p, a, b)
    f2, g2, y2, m2, f2_c, g2_c = bracket(chi_energy, c_energy, q2, p, a, b)
    sigma = lax.rsqrt(1.0 - chi_shape * y)
    sigma_sq = sigma * sigma
    psi = 1.0 - chi_energy * y2
    s = inverse(r - sigma + 1.0)
    s_sq = s * s
    s6 = s_sq * s_sq * s_sq
    t0 = s6 * (s6 - 1.0)
    t1 = s6 * s * (6.0 - 12.0 * s6)
    t2 = s6 * s_sq * (156.0 * s6 - 42.0)
    ke = (4.0 * well_depth) * e1
    kx = ke * x
    v_ee = kx * (24.0 / cutoff_sq**2)
    kxx = kx * x
    v_e = kxx * (-6.0 / cutoff_sq)
    v = kxx * x
    psi_sq = psi * psi
    psi_sq_t0 = psi_sq * t0
    psi_sq_t1 = psi_sq * t1
    u = v * psi_sq_t0
    slope = v * psi_sq_t1
    slope2 = v * psi_sq * t2
    tau = (-0.5 * chi_shape) * sigma_sq * sigma
    push = (-2.0 * chi_energy) * psi
    v_t1 = v * t1
    d1 = slope * tau
    d2 = push * (v * t0)
    h1 = p2 * d1
    h2 = p2 * d2
    kc = chi_shape * c_shape * q
    fg = chi_shape * f * g
    fg2 = chi_energy * f2 * g2
    u_a = h1 * f + h2 * f2
    u_b = h1 * g + h2 * g2
    u_fg = h1 * fg + h2 * fg2
    u_c = u * kc - u_fg
    v_e_t0 = v_e * psi_sq_t0
    d_e = r_inv * slope + v_e_t0
    u_e = d_e - (h1 * y + h2 * y2)

    p2_sq = p2 * p2
    k11 = p2_sq * (tau * (slope2 * tau + (1.5 * chi_shape) * sigma_sq * slope))
    k12 = p2_sq * (push * v_t1 * tau)
    k22 = p2_sq * ((2.0 * chi_energy * chi_energy) * (v * t0))
    steep = v_e * psi_sq_t1 + slope2 * r_inv
    l1 = p2 * (steep * tau - h1)
    l2 = p2 * (push * (v_e * t0 + v_t1 * r_inv) - h2)
    j1 = (y, f, g, fg)
    j2 = (y2, f2, g2, fg2)
    w1 = [k11 * one + k12 * two for one, two in zip(j1, j2)]
    w2 = [k12 * one + k22 * two for one, two in zip(j1, j2)]

    def quadratic(m_at, n_at):
        return w1[m_at] * j1[n_at] + w2[m_at] * j2[n_at]

    d_ee = v_ee * psi_sq_t0 + r_inv * (2.0 * (v_e * psi_sq_t1)) + p * (slope2 - slope * r_inv)
    h_ee = quadratic(0, 0) - 2.0 * (l1 * y + l2 * y2) + d_ee
    h_ea = l1 * f + l2 * f2 - quadratic(0, 1)
    h_eb = l1 * g + l2 * g2 - quadratic(0, 2)
    h_ec = quadratic(0, 3) - (l1 * fg + l2 * fg2) + kc * u_e
    straight = h1 * q + h2 * q2
    h_aa = quadratic(1, 1) + straight
    h_ab = quadratic(1, 2) - (h1 * m + h2 * m2)
    h_ac = kc * u_a - quadratic(1, 3) + (h1 * f_c + h2 * f2_c)
    h_bb = quadratic(2, 2) + straight
    h_bc = kc * u_b - quadratic(2, 3) + (h1 * g_c + h2 * g2_c)
    bent = (chi_shape * h1) * (f_c * g + f * g_c) + (chi_energy * h2) * (f2_c * g2 + f2 * g2_c)
    twist = kc * kc + (chi_shape * chi_shape) * q * (2.0 * q - 1.0)
    h_cc = quadratic(3, 3) - bent - 2.0 * (kc * u_fg) + u * twist
    gradient = (u_e, u_a, u_b, u_c)
    return gradient, (h_ee, h_ea, h_eb, h_ec, h_aa, h_ab, h_ac, h_bb, h_bc, h_cc), u_a * a + u_c * c


def offsets_of(code, period):
    return [((code >> bits & 3) - 1).astype(jnp.float32) * size for bits, size in zip((4, 2, 0), period)]


def row_of(tiles_ref, tile, k, member):
    return tiles_ref[tile, :, k * member : (k + 1) * member]


def centre_of(code, period, all_ref, member):
    shift = offsets_of(code, period)
    return [row_of(all_ref, code >> CODE_BITS, CENTRE + k, member) + shift[k] for k in range(3)]


def lanes_of(block, member):
    row = lax.broadcasted_iota(jnp.int32, (SUB, member), 0)
    lane = lax.broadcasted_iota(jnp.int32, (SUB, member), 1)
    group = (lane & -LAYER) - (block >> 1) * LAYER
    return (group & (member - 1)) + ((block & 1) * SUB + row)


def picked(block, lanes):
    return jnp.take_along_axis(block, lanes, axis=1, mode="promise_in_bounds")


def box_lanes(member):
    block = lax.broadcasted_iota(jnp.int32, (member // SUB, member), 0)
    lane = lax.broadcasted_iota(jnp.int32, (member // SUB, member), 1)
    return (((lane & -LAYER) - (block >> 1) * LAYER) & (member - 1)) + (block & 1) * SUB


def near_blocks(own_centre, partner, lanes):
    blocks, member = lanes.shape
    zero = jnp.zeros((1, member), jnp.float32)
    box = stacked(partner + [-line for line in partner] + [zero, zero])
    for bit in (1, 2, 4):
        box = jnp.maximum(box, pltpu.roll(box, member - bit, 1))

    def seen(k):
        line = jnp.broadcast_to(box[k : k + 1], (SUB, member))
        return stacked([picked(line, lanes[at : at + SUB]) for at in range(0, blocks, SUB)])

    reach = 0.0
    for k in range(3):
        above = own_centre[k] - seen(k)
        below = -own_centre[k] - seen(3 + k)
        gap = jnp.maximum(jnp.maximum(above, below), 0.0)
        reach = reach + gap * gap
    nearest = jnp.min(reach, axis=1, keepdims=True)
    weight = (1 << lax.broadcasted_iota(jnp.int32, (blocks, 1), 0)).astype(jnp.float32)
    return jnp.sum(jnp.where(nearest < cutoff_sq * 1.001, weight, 0.0)).astype(jnp.int32)


def stacked(parts):
    return jnp.concatenate(parts, axis=0)


def wide(row):
    return jnp.broadcast_to(row, (GROUP * SUB, row.shape[1]))


def partner_rows(row_at, items, lanes):
    rows = []
    for k in range(6):
        parts = []
        for item, lane in zip(items, lanes):
            row = row_at(item >> (ITEM_BITS + CODE_BITS), k)
            parts.append(picked(jnp.broadcast_to(row, lane.shape), lane))
        rows.append(stacked(parts))
    return rows


def folded(total):
    return jnp.sum(total, axis=0, keepdims=True)


def geometry(items, unused, lanes, own_code, own_wide, period, all_ref):
    member = lanes[0].shape[1]
    lane = lax.broadcasted_iota(jnp.int32, (SUB, member), 1)
    lift = []
    shifts = []
    for item, idle, other in zip(items, unused, lanes):
        code = item >> ITEM_BITS
        itself = jnp.where(other == lane, jnp.where(code == own_code, 2.0 * cutoff_sq, 0.0), 0.0)
        lift.append(itself + jnp.where(idle, 2.0 * cutoff_sq, 0.0))
        shifts.append(offsets_of(code, period))
    rows = partner_rows(lambda tile, k: row_of(all_ref, tile, CENTRE + k, member), items, lanes)
    shift = [stacked([jnp.full((SUB, member), one[k]) for one in shifts]) for k in range(3)]
    d = [rows[k] + shift[k] - own_wide[k] for k in range(3)]
    uj = rows[3:]
    gradient, hessian, spin = pair_coefficients(d, own_wide[3:], uj, stacked(lift))
    return list(gradient) + list(hessian) + d + uj, (gradient[1], spin)


def apply(moved_rows, terms, own_wide, moved_wide):
    u_e, u_a, u_b, u_c, h_ee, h_ea, h_eb, h_ec, h_aa, h_ab, h_ac, h_bb, h_bc, h_cc = terms[:14]
    d = terms[14:17]
    uj = terms[17:20]
    ui = own_wide[3:]
    dui = moved_wide[3:]
    dd = [moved_rows[k] - moved_wide[k] for k in range(3)]
    duj = cross3(moved_rows[3:], uj)
    de = dot3(d, dd)
    da = dot3(dd, ui) + dot3(d, dui)
    db = dot3(dd, uj) + dot3(d, duj)
    dc = dot3(dui, uj) + dot3(ui, duj)
    du_e = h_ee * de + h_ea * da + h_eb * db + h_ec * dc
    du_a = h_ea * de + h_aa * da + h_ab * db + h_ac * dc
    du_b = h_eb * de + h_ab * da + h_bb * db + h_bc * dc
    du_c = h_ec * de + h_ac * da + h_bc * db + h_cc * dc
    force = [du_e * d[k] + u_e * dd[k] + du_b * uj[k] + u_b * duj[k] for k in range(3)]
    turn = [du_a * d[k] + u_a * dd[k] + du_c * uj[k] + u_c * duj[k] for k in range(3)]
    return force + turn + [du_a]


def group_items(step, item_ref, item_count):
    at = [step * GROUP + part for part in range(GROUP)]
    return [item_ref[1 + place] for place in at], [place >= item_count for place in at]


def added(totals, news):
    return tuple(
        total + sum(new[part * SUB : (part + 1) * SUB] for part in range(GROUP)) for total, new in zip(totals, news)
    )


def close(sums, kept, spin, u, t):
    force = [-(sums[k] + u[k] * sums[6] + t[k] * kept) for k in range(3)]
    return force + list(cross3(u, [sums[3 + k] - t[k] * spin for k in range(3)]))


def spread(rows, out_ref):
    member = rows[0].shape[1]
    for k, row in enumerate(rows):
        out_ref[:, :, k * member : (k + 1) * member] = jnp.broadcast_to(row[None], (out_ref.shape[0], 1, member))


def pack_kernel(*refs):
    sources, out_ref, targets, sems = refs[:4], refs[4], refs[5:9], refs[9]
    config_ref, start_ref, list_ref, count_ref = targets
    copies = [
        pltpu.make_async_copy(source, target, sems.at[at]) for at, (source, target) in enumerate(zip(sources, targets))
    ]
    for copy in copies:
        copy.start()
    copies[2].wait()
    copies[3].wait()
    member = config_ref.shape[1]
    lane = lax.broadcasted_iota(jnp.int32, (1, member), 1)
    fields, slots = list_ref.shape[1], list_ref.shape[3]
    line = jnp.full((1, member), -9, jnp.int32)
    for field in range(fields):
        for slot in range(slots):
            line = jnp.where(lane == field * slots + slot, list_ref[0, field, 0, slot], line)
    line = jnp.where((lane >= count_ref[0, 0]) & (lane < slots), -9, line).astype(jnp.float32)
    copies[0].wait()
    copies[1].wait()
    rows = [ref[k : k + 1, :] for ref in (start_ref, config_ref) for k in range(6)]
    spread(rows + [line], out_ref)


def first_kernel(
    rows,
    cols,
    slots,
    period,
    all_ref,
    out_ref,
    item_ref,
    coef_ref,
    kept_ref,
    entry_ref,
    code_ref,
    code_smem,
    sem,
):
    member = kept_ref.shape[1]
    row_id = lax.axis_index("row")
    col_id = lax.axis_index("col")
    own = row_id * cols + col_id
    blocks = member // SUB

    def field(line, at):
        return line if at == 0 else pltpu.roll(line, member - at * slots, 1)

    row_f = row_id.astype(jnp.float32)
    col_f = col_id.astype(jnp.float32)
    lines = [row_of(all_ref, row_id * cols + col, LIST_ROW, member) for col in range(cols)]
    lines += [row_of(all_ref, row * cols + col_id, LIST_ROW, member) for row in range(rows)]
    line = jnp.concatenate(lines, axis=0)
    at = lax.broadcasted_iota(jnp.int32, line.shape, 0).astype(jnp.float32)
    near = at < float(cols)
    other = field(line, 1)
    offset = field(line, 2) * 16.0 + field(line, 3) * 4.0 + field(line, 4)
    partner = jnp.where(near, other * float(cols) + at, (at - float(cols)) * float(cols) + line)
    code = partner * float(1 << CODE_BITS) + (jnp.where(near, offset, -offset) + 21.0)
    hit = jnp.where(near, line - col_f, jnp.where(line >= 0.0, other - row_f, 1.0)) == 0.0
    code_ref[...] = jnp.where(hit, code, -1.0).astype(jnp.int32)
    copy = pltpu.make_async_copy(code_ref, code_smem, sem)
    copy.start()
    own_code = own * (1 << CODE_BITS) + 21
    own_moved = [row_of(all_ref, own, k, member) for k in range(6)]
    own_frame = [row_of(all_ref, own, CENTRE + k, member) for k in range(6)]
    lanes = box_lanes(member)
    own_centre = [jnp.broadcast_to(line, lanes.shape) for line in own_frame[:3]]

    def append(code, bits, count):
        for block in range(blocks):
            item_ref[1 + count] = (code << ITEM_BITS) + block
            count = count + (bits >> block & 1)
        return count

    items = append(own_code, near_blocks(own_centre, own_frame[:3], lanes), jnp.int32(0))
    copy.wait()

    def gather(line, count):
        for slot in range(slots):
            code = code_smem[line, slot]
            entry_ref[count] = code
            count = count + (code >= 0).astype(jnp.int32)
        return count

    entries = lax.fori_loop(0, rows + cols, gather, jnp.int32(0))
    for part in range(TESTS):
        entry_ref[entries + part] = own_code

    def prepare(step, count):
        codes = [entry_ref[step * TESTS + part] for part in range(TESTS)]
        bits = [near_blocks(own_centre, centre_of(code, period, all_ref, member), lanes) for code in codes]
        for part in range(TESTS):
            count = append(codes[part], jnp.where(step * TESTS + part < entries, bits[part], 0), count)
        return count

    items = lax.fori_loop(0, (entries + TESTS - 1) // TESTS, prepare, items)
    for part in range(GROUP):
        item_ref[1 + items + part] = own_code << ITEM_BITS
    item_ref[0] = items

    held = coef_ref.shape[0] // (TERMS * GROUP * SUB)
    steps = (items + GROUP - 1) // GROUP
    u = own_frame[3:]
    t = cross3(own_moved[3:], u)
    own_wide = [wide(line) for line in own_frame]
    moved_wide = [wide(line) for line in [*own_moved[:3], *t]]

    def derive(step, totals):
        group, unused = group_items(step, item_ref, items)
        lanes = [lanes_of(item & ITEM_MASK, member) for item in group]
        terms, sums = geometry(group, unused, lanes, own_code, own_wide, period, all_ref)
        moved_rows = partner_rows(lambda tile, k: row_of(all_ref, tile, k, member), group, lanes)
        return terms, added(totals, apply(moved_rows, terms, own_wide, moved_wide) + list(sums))

    def keep(step, totals):
        terms, totals = derive(step, totals)
        start = pl.multiple_of(step * (TERMS * GROUP * SUB), SUB)
        for k in range(TERMS):
            coef_ref[pl.ds(start + k * GROUP * SUB, GROUP * SUB), :] = terms[k]
        return totals

    zero = jnp.zeros((SUB, member), jnp.float32)
    totals = lax.fori_loop(0, jnp.minimum(steps, held), keep, (zero,) * 9)
    totals = lax.fori_loop(held, steps, lambda step, before: derive(step, before)[1], totals)
    sums = [folded(total) for total in totals]
    kept_ref[...] = jnp.concatenate(sums[7:], axis=0)
    spread(close(sums, sums[7], sums[8], u, t), out_ref)


def scalar_of(block):
    return jnp.sum(jnp.sum(block, axis=0, keepdims=True), axis=1, keepdims=True)


def second_kernel(
    cols,
    total_entries,
    period,
    item_ref,
    coef_ref,
    kept_ref,
    all_ref,
    image_ref,
    out_ref,
    pair_ref,
    scalar_ref,
    second_ref,
):
    own = lax.axis_index("row") * cols + lax.axis_index("col")
    member = kept_ref.shape[1]
    basis = all_ref[:, 0, 0 : 6 * member]
    image = image_ref[:, 0, :]
    portion = 1.0 / total_entries

    def total_of(block):
        return scalar_of(sum(block[:, k * member : (k + 1) * member] for k in range(6)))

    norm_sq = total_of(basis * basis) * portion + norm_eps
    norm_inv = lax.rsqrt(norm_sq)
    alpha = total_of(basis * image) * portion / norm_sq
    second = image - alpha * basis
    second_ref[:, 0, :] = second
    beta_sq = total_of(second * second) * portion / norm_sq + norm_eps
    beta = jnp.sqrt(beta_sq)
    scale = norm_inv * lax.rsqrt(beta_sq)

    own_code = own * (1 << CODE_BITS) + 21
    items = item_ref[0]
    held = coef_ref.shape[0] // (TERMS * GROUP * SUB)
    steps = (items + GROUP - 1) // GROUP

    def moved_row(tile, k):
        return row_of(second_ref, tile, k, member)

    own_moved = [moved_row(own, k) for k in range(6)]
    own_frame = [row_of(all_ref, own, CENTRE + k, member) for k in range(6)]
    u = own_frame[3:]
    t = cross3(own_moved[3:], u)
    own_wide = [wide(line) for line in own_frame]
    moved_wide = [wide(line) for line in [*own_moved[:3], *t]]

    def visit(step, totals):
        group, _ = group_items(step, item_ref, items)
        lanes = [lanes_of(item & ITEM_MASK, member) for item in group]
        start = pl.multiple_of(step * (TERMS * GROUP * SUB), SUB)
        terms = [coef_ref[pl.ds(start + k * GROUP * SUB, GROUP * SUB), :] for k in range(TERMS)]
        return added(totals, apply(partner_rows(moved_row, group, lanes), terms, own_wide, moved_wide))

    def visit_again(step, totals):
        group, unused = group_items(step, item_ref, items)
        lanes = [lanes_of(item & ITEM_MASK, member) for item in group]
        terms, _ = geometry(group, unused, lanes, own_code, own_wide, period, all_ref)
        return added(totals, apply(partner_rows(moved_row, group, lanes), terms, own_wide, moved_wide))

    zero = jnp.zeros((SUB, member), jnp.float32)
    totals = lax.fori_loop(0, jnp.minimum(steps, held), visit, (zero,) * 7)
    totals = lax.fori_loop(held, steps, visit_again, totals)
    sums = [folded(total) for total in totals]
    product = close(sums, kept_ref[0:1, :], kept_ref[1:2, :], u, t)
    fill = [jnp.zeros((1, member), jnp.float32)] * (SUB - len(product))
    first = stacked([row_of(all_ref, own, k, member) for k in range(6)] + fill)
    image = stacked(product + fill) * scale - (beta * norm_inv) * first
    second = stacked(own_moved + fill) * scale
    inner = scalar_of(second * image)
    weight = scalar_of(second * second)
    local_alpha = jnp.where(weight > 1e-30, inner / jnp.maximum(weight, 1e-30), 0.0)
    rest = image - local_alpha * second
    size = scalar_of(rest * rest)
    slant = scalar_of(second * rest)
    lane = lax.broadcasted_iota(jnp.int32, (1, member), 1)
    line = jnp.zeros((1, member), jnp.float32)
    for at, value in enumerate((inner, weight, local_alpha, size, slant)):
        line = jnp.where(lane == at, value, line)
    out_ref[...] = jnp.broadcast_to(line[None], out_ref.shape)
    pair_ref[0] = second
    pair_ref[1] = image
    scalar_ref[...] = jnp.where(lane == 0, alpha, jnp.where(lane == 1, beta, 0.0))


def last_kernel(total_entries, pair_ref, scalar_ref, line_ref, mode_ref, coefficient_ref):
    lines = line_ref[:, 0, :]
    alpha = jnp.sum(lines[:, 0:1], axis=0, keepdims=True) / total_entries
    away = lines[:, 2:3] - alpha
    parts = lines[:, 3:4] + away * (away * lines[:, 1:2] + 2.0 * lines[:, 4:5])
    beta = jnp.sqrt(jnp.sum(parts, axis=0, keepdims=True) / total_entries + norm_eps)
    mode = (pair_ref[1] - alpha * pair_ref[0]) / beta
    mode_ref[...] = mode[: mode_ref.shape[0]]
    for at, value in enumerate((scalar_ref[0:1, 0:1], scalar_ref[0:1, 1:2], alpha, beta)):
        coefficient_ref[at] = jnp.sum(value)


def local(config, start, tile_list, tile_count):
    dof, member = config.shape
    row_devices = lax.axis_size("row")
    col_devices = lax.axis_size("col")
    devices = row_devices * col_devices
    total_entries = float(dof * member * devices)
    period = (5.0, 5.0, 3.5 * (member // 16))
    slots = tile_list.shape[2]
    longest = (row_devices + col_devices) * slots + 1

    def shaped(*shape):
        return jax.ShapeDtypeStruct(shape, jnp.float32)

    def everywhere(copies):
        return lax.all_to_all(copies, ("row", "col"), 0, 0, tiled=True)

    params = pltpu.CompilerParams(vmem_limit_bytes=VMEM_LIMIT)
    vmem = pl.BlockSpec(memory_space=pltpu.VMEM)
    smem = pl.BlockSpec(memory_space=pltpu.SMEM)

    outside = pl.BlockSpec(memory_space=pl.ANY)
    packed = pl.pallas_call(
        pack_kernel,
        out_shape=shaped(devices, 1, (LIST_ROW + 1) * member),
        in_specs=[outside] * 4,
        out_specs=vmem,
        scratch_shapes=[
            pltpu.VMEM((dof, member), jnp.float32),
            pltpu.VMEM((dof, member), jnp.float32),
            pltpu.SMEM((1, tile_list.shape[3], 1, slots), jnp.int32),
            pltpu.SMEM((1, 1), jnp.int32),
            pltpu.SemaphoreType.DMA((4,)),
        ],
        compiler_params=pltpu.CompilerParams(vmem_limit_bytes=PACK_LIMIT),
    )(config, start, jnp.transpose(tile_list, (0, 3, 1, 2)), tile_count)
    together = everywhere(packed)

    held_rows = HELD // GROUP * (TERMS * GROUP * SUB)
    image, items, terms, kept = pl.pallas_call(
        functools.partial(first_kernel, row_devices, col_devices, slots, period),
        out_shape=(
            shaped(devices, 1, dof * member),
            jax.ShapeDtypeStruct((1 + longest * (member // SUB) + GROUP,), jnp.int32),
            shaped(held_rows, member),
            shaped(2, member),
        ),
        in_specs=[vmem],
        out_specs=(vmem, smem, vmem, vmem),
        scratch_shapes=[
            pltpu.SMEM((longest + TESTS,), jnp.int32),
            pltpu.VMEM((row_devices + col_devices, member), jnp.int32),
            pltpu.SMEM((row_devices + col_devices, member), jnp.int32),
            pltpu.SemaphoreType.DMA,
        ],
        compiler_params=params,
    )(together)
    image = everywhere(image)

    line, pair, scalars = pl.pallas_call(
        functools.partial(second_kernel, col_devices, total_entries, period),
        out_shape=(shaped(devices, 1, member), shaped(2, SUB, member), shaped(1, member)),
        in_specs=[smem] + [vmem] * 4,
        out_specs=(vmem, vmem, vmem),
        scratch_shapes=[
            pltpu.VMEM((devices, 1, dof * member), jnp.float32),
        ],
        compiler_params=params,
    )(items, terms, kept, together, image)
    line = everywhere(line)

    mode, coefficients = pl.pallas_call(
        functools.partial(last_kernel, total_entries),
        out_shape=(shaped(dof, member), shaped(4)),
        in_specs=[vmem] * 3,
        out_specs=(vmem, smem),
        compiler_params=params,
    )(pair, scalars, line)
    return (coefficients, mode)


def solution(mesh):
    placed = (
        P(None, ("row", "col")),
        P(None, ("row", "col")),
        P("row", "col", None, None),
        P("row", "col"),
    )
    return jax.shard_map(
        local, mesh=mesh, in_specs=placed, out_specs=(P(), P(None, ("row", "col"))), check_vma=False
    )
```

profile of v0, /device:TPU:0, one launch (start us, length us, event | category | flops | bytes accessed | tf_op | source)
XLA Modules:
  0.0 46.2 jit_solution(3723920727468737919)
XLA Ops:
  1.3 1.7 %shard_map.59 = f32[32,1,1664]{2,1,0:T(1,128)} custom-call(f32[6,128]{1,0:T(8,128)} %refs_0_.1, f32[6,128]{1,0:T(8,128)} %refs_1_.1, s32[1,5,1,8]{3,2,1,0:T(1,128)} %bitcast.1, s32[1,1]{1,0:T(1,128)S(6)} %copy.6.refs_3_), custom_call_target="tpu_custom_call" | custom-call | tf_op jit(solution)/shard_map/pallas_call | solution.py:536
  3.0 16.7 %all_to_all.15.all_ref = f32[32,1,1664]{2,1,0:T(1,128)S(1)} all-to-all(f32[32,1,1664]{2,1,0:T(1,128)} %shard_map.59), channel_id=1, replica_groups=mesh['row'=4,'col'=8] {'row','col'}, dimensions={0} | all-to-all | bytes 425984 | tf_op jit(solution)/shard_map/all_to_all | solution.py:529
  19.7 4.6 %shard_map.60 = (f32[32,1,768]{2,1,0:T(1,128)S(1)}, s32[1557]{0:T(1024)S(1)}, f32[20480,128]{1,0:T(8,128)S(1)}, f32[2,128]{1,0:T(2,128)S(1)}) custom-call(f32[32,1,1664]{2,1,0:T(1,128)S(1)} %all_to_all.15.all_ref), custom_call_target="tpu_custom_call" | custom-call | tf_op jit(solution)/shard_map/pallas_call | solution.py:553
  24.3 10.2 %all_to_all.16.image_ref = f32[32,1,768]{2,1,0:T(1,128)S(1)} all-to-all(f32[32,1,768]{2,1,0:T(1,128)S(1)} %get-tuple-element.14), channel_id=1, replica_groups=mesh['row'=4,'col'=8] {'row','col'}, dimensions={0} | all-to-all | bytes 196608 | tf_op jit(solution)/shard_map/all_to_all | solution.py:529
  34.5 2.0 %shard_map.61 = (f32[32,1,128]{2,1,0:T(1,128)S(1)}, f32[2,8,128]{2,1,0:T(8,128)S(1)}, f32[1,128]{1,0:T(1,128)S(1)}) custom-call(s32[1557]{0:T(1024)S(1)} %get-tuple-element.11.item_ref, f32[20480,128]{1,0:T(8,128)S(1)} %get-tuple-element.12.coef_ref, f32[2,128]{1,0:T(2,128)S(1)} %get-tuple-element.13.kept_ref, f32[32,1,1664]{2,1,0:T(1,128)S(1)} %all_to_all.15.all_ref, ...), custom_call_target="tpu_custom_call" | custom-call | tf_op jit(solution)/shard_map/pallas_call | solution.py:573
  36.5 8.8 %all_to_all.17.line_ref = f32[32,1,128]{2,1,0:T(1,128)S(1)} all-to-all(f32[32,1,128]{2,1,0:T(1,128)S(1)} %get-tuple-element.17), channel_id=1, replica_groups=mesh['row'=4,'col'=8] {'row','col'}, dimensions={0} | all-to-all | bytes 32768 | tf_op jit(solution)/shard_map/all_to_all | solution.py:529
  45.4 0.8 %shard_map.62 = (f32[6,128]{1,0:T(8,128)}, f32[4]{0:T(128)}) custom-call(f32[2,8,128]{2,1,0:T(8,128)S(1)} %get-tuple-element.15.pair_ref, f32[1,128]{1,0:T(1,128)S(1)} %get-tuple-element.16.scalar_ref, f32[32,1,128]{2,1,0:T(1,128)S(1)} %all_to_all.17.line_ref), custom_call_target="tpu_custom_call" | custom-call | tf_op jit(solution)/shard_map/pallas_call | solution.py:585
where the time goes:
time: 46.6 us; the launch traced here: 46.2 us
  blocking collectives  35.8 us (77%)
  Pallas kernels  9.13 us (20%)
  between operations  1.3 us (3%)
    all_to_all x3, blocking collectives, everywhere(): return lax.all_to_all(copies, ('row', 'col'), 0, 0, tiled=True)  35.8 us
    pallas_call x1, Pallas kernels, local(): pl.pallas_call(functools.partial(first_kernel, row_devices, col_devices,...  4.65 us
    pallas_call x1, Pallas kernels, local(): pl.pallas_call(functools.partial(second_kernel, col_devices, total_entrie...  1.99 us
    pallas_call x1, Pallas kernels, local(): pl.pallas_call(pack_kernel, out_shape=shaped(devices, 1, (LIST_ROW + 1) *...  1.69 us

commit v1 on v0

--- a/solution.py
+++ b/solution.py
@@ -19,6 +19,7 @@
 LIST_ROW = 12
 CODE_BITS = 6
 ITEM_BITS = 8
+BLOCK_BITS = 16
 ITEM_MASK = 255
 LAYER = 16
 TESTS = 5
@@ -259,9 +260,16 @@
     return force + turn + [du_a]
 
 
+def append(item_ref, code, bits, count, blocks):
+    for block in range(blocks):
+        item_ref[count] = (code << ITEM_BITS) + block
+        count = count + (bits >> block & 1)
+    return count
+
+
 def group_items(step, item_ref, item_count):
     at = [step * GROUP + part for part in range(GROUP)]
-    return [item_ref[1 + place] for place in at], [place >= item_count for place in at]
+    return [item_ref[place] for place in at], [place >= item_count for place in at]
 
 
 def added(totals, news):
@@ -312,10 +320,10 @@
     period,
     all_ref,
     out_ref,
-    item_ref,
+    entry_ref,
     coef_ref,
     kept_ref,
-    entry_ref,
+    item_ref,
     code_ref,
     code_smem,
     sem,
@@ -341,7 +349,16 @@
     partner = jnp.where(near, other * float(cols) + at, (at - float(cols)) * float(cols) + line)
     code = partner * float(1 << CODE_BITS) + (jnp.where(near, offset, -offset) + 21.0)
     hit = jnp.where(near, line - col_f, jnp.where(line >= 0.0, other - row_f, 1.0)) == 0.0
-    code_ref[...] = jnp.where(hit, code, -1.0).astype(jnp.int32)
+    found = jnp.where(hit, code + 1.0, 0.0)
+    found = jnp.where(lax.broadcasted_iota(jnp.int32, found.shape, 1) < slots, found, 0.0)
+    held_lines = member // slots
+    for group in range(code_ref.shape[0]):
+        packed = -1.0
+        for at in range(group * held_lines, min((group + 1) * held_lines, rows + cols)):
+            part = found[at : at + 1]
+            by = (at - group * held_lines) * slots
+            packed = packed + (pltpu.roll(part, by, 1) if by else part)
+        code_ref[group : group + 1, :] = packed.astype(jnp.int32)
     copy = pltpu.make_async_copy(code_ref, code_smem, sem)
     copy.start()
     own_code = own * (1 << CODE_BITS) + 21
@@ -350,37 +367,38 @@
     lanes = box_lanes(member)
     own_centre = [jnp.broadcast_to(line, lanes.shape) for line in own_frame[:3]]
 
-    def append(code, bits, count):
-        for block in range(blocks):
-            item_ref[1 + count] = (code << ITEM_BITS) + block
-            count = count + (bits >> block & 1)
-        return count
-
-    items = append(own_code, near_blocks(own_centre, own_frame[:3], lanes), jnp.int32(0))
+    own_bits = near_blocks(own_centre, own_frame[:3], lanes)
+    entry_ref[1] = (own_code << BLOCK_BITS) + own_bits
+    items = append(item_ref, own_code, own_bits, jnp.int32(0), blocks)
     copy.wait()
 
-    def gather(line, count):
+    def gather(group, at, count):
         for slot in range(slots):
-            code = code_smem[line, slot]
-            entry_ref[count] = code
+            code = code_smem[group, at * slots + slot]
+            entry_ref[2 + count] = code
             count = count + (code >= 0).astype(jnp.int32)
         return count
 
-    entries = lax.fori_loop(0, rows + cols, gather, jnp.int32(0))
+    entries = jnp.int32(0)
+    for group in range(code_ref.shape[0]):
+        some = min(held_lines, rows + cols - group * held_lines)
+        entries = lax.fori_loop(0, some, functools.partial(gather, group), entries)
     for part in range(TESTS):
-        entry_ref[entries + part] = own_code
+        entry_ref[2 + entries + part] = own_code
 
     def prepare(step, count):
-        codes = [entry_ref[step * TESTS + part] for part in range(TESTS)]
+        codes = [entry_ref[2 + step * TESTS + part] for part in range(TESTS)]
         bits = [near_blocks(own_centre, centre_of(code, period, all_ref, member), lanes) for code in codes]
         for part in range(TESTS):
-            count = append(codes[part], jnp.where(step * TESTS + part < entries, bits[part], 0), count)
+            some = jnp.where(step * TESTS + part < entries, bits[part], 0)
+            entry_ref[2 + step * TESTS + part] = (codes[part] << BLOCK_BITS) + some
+            count = append(item_ref, codes[part], some, count, blocks)
         return count
 
     items = lax.fori_loop(0, (entries + TESTS - 1) // TESTS, prepare, items)
+    entry_ref[0] = entries + 1
     for part in range(GROUP):
-        item_ref[1 + items + part] = own_code << ITEM_BITS
-    item_ref[0] = items
+        item_ref[items + part] = own_code << ITEM_BITS
 
     held = coef_ref.shape[0] // (TERMS * GROUP * SUB)
     steps = (items + GROUP - 1) // GROUP
@@ -419,7 +437,7 @@
     cols,
     total_entries,
     period,
-    item_ref,
+    entry_ref,
     coef_ref,
     kept_ref,
     all_ref,
@@ -428,6 +446,7 @@
     pair_ref,
     scalar_ref,
     second_ref,
+    item_ref,
 ):
     own = lax.axis_index("row") * cols + lax.axis_index("col")
     member = kept_ref.shape[1]
@@ -448,7 +467,15 @@
     scale = norm_inv * lax.rsqrt(beta_sq)
 
     own_code = own * (1 << CODE_BITS) + 21
-    items = item_ref[0]
+    blocks = member // SUB
+
+    def relist(entry, count):
+        word = entry_ref[1 + entry]
+        return append(item_ref, word >> BLOCK_BITS, word & ((1 << BLOCK_BITS) - 1), count, blocks)
+
+    items = lax.fori_loop(0, entry_ref[0], relist, jnp.int32(0))
+    for part in range(GROUP):
+        item_ref[items + part] = own_code << ITEM_BITS
     held = coef_ref.shape[0] // (TERMS * GROUP * SUB)
     steps = (items + GROUP - 1) // GROUP
 
@@ -549,21 +576,23 @@
     )(config, start, jnp.transpose(tile_list, (0, 3, 1, 2)), tile_count)
     together = everywhere(packed)
 
+    item_list = pltpu.SMEM((longest * (member // SUB) + GROUP,), jnp.int32)
+    code_rows = -(-(row_devices + col_devices) * slots // member)
     held_rows = HELD // GROUP * (TERMS * GROUP * SUB)
-    image, items, terms, kept = pl.pallas_call(
+    image, entries, terms, kept = pl.pallas_call(
         functools.partial(first_kernel, row_devices, col_devices, slots, period),
         out_shape=(
             shaped(devices, 1, dof * member),
-            jax.ShapeDtypeStruct((1 + longest * (member // SUB) + GROUP,), jnp.int32),
+            jax.ShapeDtypeStruct((1 + longest + TESTS,), jnp.int32),
             shaped(held_rows, member),
             shaped(2, member),
         ),
         in_specs=[vmem],
         out_specs=(vmem, smem, vmem, vmem),
         scratch_shapes=[
-            pltpu.SMEM((longest + TESTS,), jnp.int32),
-            pltpu.VMEM((row_devices + col_devices, member), jnp.int32),
-            pltpu.SMEM((row_devices + col_devices, member), jnp.int32),
+            item_list,
+            pltpu.VMEM((code_rows, member), jnp.int32),
+            pltpu.SMEM((code_rows, member), jnp.int32),
             pltpu.SemaphoreType.DMA,
         ],
         compiler_params=params,
@@ -577,9 +606,10 @@
         out_specs=(vmem, vmem, vmem),
         scratch_shapes=[
             pltpu.VMEM((devices, 1, dof * member), jnp.float32),
+            item_list,
         ],
         compiler_params=params,
-    )(items, terms, kept, together, image)
+    )(entries, terms, kept, together, image)
     line = everywhere(line)
 
     mode, coefficients = pl.pallas_call(

time: 46.6 us -> 48.1 us (1.032)
  blocking collectives: 35.8 us -> 37.1 us
  Pallas kernels: 9.13 us -> 9.68 us
    all_to_all x3, blocking collectives: 35.8 us -> 37.1 us  [everywhere(): return lax.all_to_all(copies, ('row', 'col'), 0, 0, tiled=True)]
    pallas_call x1, Pallas kernels: 4.65 us -> 5.15 us  [local(): pl.pallas_call(functools.partial(first_kernel, row_devices, col_devices,...]
where the time goes in v1:
time: 48.1 us; the launch traced here: 48 us
  blocking collectives  37.1 us (77%)
  Pallas kernels  9.68 us (20%)
  between operations  1.3 us (3%)
    all_to_all x3, blocking collectives, everywhere(): return lax.all_to_all(copies, ('row', 'col'), 0, 0, tiled=True)  37.1 us
    pallas_call x1, Pallas kernels, local(): pl.pallas_call(functools.partial(first_kernel, row_devices, col_devices,...  5.15 us
    pallas_call x1, Pallas kernels, local(): pl.pallas_call(functools.partial(second_kernel, col_devices, total_entrie...  2.04 us
    pallas_call x1, Pallas kernels, local(): pl.pallas_call(pack_kernel, out_shape=shaped(devices, 1, (LIST_ROW + 1) *...  1.69 us

profile of v1, /device:TPU:0, one launch (start us, length us, event | category | flops | bytes accessed | tf_op | source)
XLA Modules:
  0.0 48.0 jit_solution(14481101937198881747)
XLA Ops:
  1.3 1.7 %shard_map.59 = f32[32,1,1664]{2,1,0:T(1,128)} custom-call(f32[6,128]{1,0:T(8,128)} %refs_0_.1, f32[6,128]{1,0:T(8,128)} %refs_1_.1, s32[1,5,1,8]{3,2,1,0:T(1,128)} %bitcast.1, s32[1,1]{1,0:T(1,128)S(6)} %copy.6.refs_3_), custom_call_target="tpu_custom_call" | custom-call | tf_op jit(solution)/shard_map/pallas_call | solution.py:563
  3.0 16.7 %all_to_all.15.all_ref = f32[32,1,1664]{2,1,0:T(1,128)S(1)} all-to-all(f32[32,1,1664]{2,1,0:T(1,128)} %shard_map.59), channel_id=1, replica_groups=mesh['row'=4,'col'=8] {'row','col'}, dimensions={0} | all-to-all | bytes 425984 | tf_op jit(solution)/shard_map/all_to_all | solution.py:556
  19.7 5.1 %shard_map.60 = (f32[32,1,768]{2,1,0:T(1,128)S(1)}, s32[103]{0:T(128)S(1)}, f32[20480,128]{1,0:T(8,128)S(1)}, f32[2,128]{1,0:T(2,128)S(1)}) custom-call(f32[32,1,1664]{2,1,0:T(1,128)S(1)} %all_to_all.15.all_ref), custom_call_target="tpu_custom_call" | custom-call | tf_op jit(solution)/shard_map/pallas_call | solution.py:582
  24.8 11.5 %all_to_all.16.image_ref = f32[32,1,768]{2,1,0:T(1,128)S(1)} all-to-all(f32[32,1,768]{2,1,0:T(1,128)S(1)} %get-tuple-element.14), channel_id=1, replica_groups=mesh['row'=4,'col'=8] {'row','col'}, dimensions={0} | all-to-all | bytes 196608 | tf_op jit(solution)/shard_map/all_to_all | solution.py:556
  36.3 2.0 %shard_map.61 = (f32[32,1,128]{2,1,0:T(1,128)S(1)}, f32[2,8,128]{2,1,0:T(8,128)S(1)}, f32[1,128]{1,0:T(1,128)S(1)}) custom-call(s32[103]{0:T(128)S(1)} %get-tuple-element.11.entry_ref, f32[20480,128]{1,0:T(8,128)S(1)} %get-tuple-element.12.coef_ref, f32[2,128]{1,0:T(2,128)S(1)} %get-tuple-element.13.kept_ref, f32[32,1,1664]{2,1,0:T(1,128)S(1)} %all_to_all.15.all_ref, ...), custom_call_target="tpu_custom_call" | custom-call | tf_op jit(solution)/shard_map/pallas_call | solution.py:602
  38.4 8.8 %all_to_all.17.line_ref = f32[32,1,128]{2,1,0:T(1,128)S(1)} all-to-all(f32[32,1,128]{2,1,0:T(1,128)S(1)} %get-tuple-element.17), channel_id=1, replica_groups=mesh['row'=4,'col'=8] {'row','col'}, dimensions={0} | all-to-all | bytes 32768 | tf_op jit(solution)/shard_map/all_to_all | solution.py:556
  47.2 0.8 %shard_map.62 = (f32[6,128]{1,0:T(8,128)}, f32[4]{0:T(128)}) custom-call(f32[2,8,128]{2,1,0:T(8,128)S(1)} %get-tuple-element.15.pair_ref, f32[1,128]{1,0:T(1,128)S(1)} %get-tuple-element.16.scalar_ref, f32[32,1,128]{2,1,0:T(1,128)S(1)} %all_to_all.17.line_ref), custom_call_target="tpu_custom_call" | custom-call | tf_op jit(solution)/shard_map/pallas_call | solution.py:615

commit v2 on v0

--- a/solution.py
+++ b/solution.py
@@ -201,8 +201,8 @@
     return jnp.concatenate(parts, axis=0)
 
 
-def wide(row):
-    return jnp.broadcast_to(row, (GROUP * SUB, row.shape[1]))
+def wide(row, blocks=GROUP):
+    return jnp.broadcast_to(row, (blocks * SUB, row.shape[1]))
 
 
 def partner_rows(row_at, items, lanes):
@@ -266,7 +266,7 @@
 
 def added(totals, news):
     return tuple(
-        total + sum(new[part * SUB : (part + 1) * SUB] for part in range(GROUP)) for total, new in zip(totals, news)
+        total + sum(new[at : at + SUB] for at in range(0, new.shape[0], SUB)) for total, new in zip(totals, news)
     )
 
 
@@ -382,30 +382,25 @@
         item_ref[1 + items + part] = own_code << ITEM_BITS
     item_ref[0] = items
 
-    held = coef_ref.shape[0] // (TERMS * GROUP * SUB)
+    spare = coef_ref.shape[0] // (TERMS * GROUP * SUB) - 1
     steps = (items + GROUP - 1) // GROUP
     u = own_frame[3:]
     t = cross3(own_moved[3:], u)
     own_wide = [wide(line) for line in own_frame]
     moved_wide = [wide(line) for line in [*own_moved[:3], *t]]
 
-    def derive(step, totals):
+    def keep(step, totals):
         group, unused = group_items(step, item_ref, items)
         lanes = [lanes_of(item & ITEM_MASK, member) for item in group]
         terms, sums = geometry(group, unused, lanes, own_code, own_wide, period, all_ref)
         moved_rows = partner_rows(lambda tile, k: row_of(all_ref, tile, k, member), group, lanes)
-        return terms, added(totals, apply(moved_rows, terms, own_wide, moved_wide) + list(sums))
-
-    def keep(step, totals):
-        terms, totals = derive(step, totals)
-        start = pl.multiple_of(step * (TERMS * GROUP * SUB), SUB)
+        start = pl.multiple_of(jnp.minimum(step, spare) * (TERMS * GROUP * SUB), SUB)
         for k in range(TERMS):
             coef_ref[pl.ds(start + k * GROUP * SUB, GROUP * SUB), :] = terms[k]
-        return totals
+        return added(totals, apply(moved_rows, terms, own_wide, moved_wide) + list(sums))
 
     zero = jnp.zeros((SUB, member), jnp.float32)
-    totals = lax.fori_loop(0, jnp.minimum(steps, held), keep, (zero,) * 9)
-    totals = lax.fori_loop(held, steps, lambda step, before: derive(step, before)[1], totals)
+    totals = lax.fori_loop(0, steps, keep, (zero,) * 9)
     sums = [folded(total) for total in totals]
     kept_ref[...] = jnp.concatenate(sums[7:], axis=0)
     spread(close(sums, sums[7], sums[8], u, t), out_ref)
@@ -449,7 +444,7 @@
 
     own_code = own * (1 << CODE_BITS) + 21
     items = item_ref[0]
-    held = coef_ref.shape[0] // (TERMS * GROUP * SUB)
+    held = coef_ref.shape[0] // (TERMS * GROUP * SUB) - 1
     steps = (items + GROUP - 1) // GROUP
 
     def moved_row(tile, k):
@@ -469,15 +464,18 @@
         terms = [coef_ref[pl.ds(start + k * GROUP * SUB, GROUP * SUB), :] for k in range(TERMS)]
         return added(totals, apply(partner_rows(moved_row, group, lanes), terms, own_wide, moved_wide))
 
-    def visit_again(step, totals):
-        group, unused = group_items(step, item_ref, items)
-        lanes = [lanes_of(item & ITEM_MASK, member) for item in group]
-        terms, _ = geometry(group, unused, lanes, own_code, own_wide, period, all_ref)
-        return added(totals, apply(partner_rows(moved_row, group, lanes), terms, own_wide, moved_wide))
+    own_once = [wide(line, 1) for line in own_frame]
+    moved_once = [wide(line, 1) for line in [*own_moved[:3], *t]]
+
+    def visit_again(place, totals):
+        item = item_ref[1 + place]
+        lanes = lanes_of(item & ITEM_MASK, member)
+        terms, _ = geometry([item], [False], [lanes], own_code, own_once, period, all_ref)
+        return added(totals, apply(partner_rows(moved_row, [item], [lanes]), terms, own_once, moved_once))
 
     zero = jnp.zeros((SUB, member), jnp.float32)
     totals = lax.fori_loop(0, jnp.minimum(steps, held), visit, (zero,) * 7)
-    totals = lax.fori_loop(held, steps, visit_again, totals)
+    totals = lax.fori_loop(held * GROUP, items, visit_again, totals)
     sums = [folded(total) for total in totals]
     product = close(sums, kept_ref[0:1, :], kept_ref[1:2, :], u, t)
     fill = [jnp.zeros((1, member), jnp.float32)] * (SUB - len(product))
@@ -549,7 +547,7 @@
     )(config, start, jnp.transpose(tile_list, (0, 3, 1, 2)), tile_count)
     together = everywhere(packed)
 
-    held_rows = HELD // GROUP * (TERMS * GROUP * SUB)
+    held_rows = (HELD // GROUP + 1) * (TERMS * GROUP * SUB)
     image, items, terms, kept = pl.pallas_call(
         functools.partial(first_kernel, row_devices, col_devices, slots, period),
         out_shape=(

time: 46.6 us -> 47.7 us (1.024)
  Pallas kernels: 9.13 us -> 10.4 us
    pallas_call x1, Pallas kernels: 4.65 us -> 5.73 us  [local(): pl.pallas_call(functools.partial(first_kernel, row_devices, col_devices,...]
where the time goes in v2:
time: 47.7 us; the launch traced here: 47.3 us
  blocking collectives  35.6 us (75%)
  Pallas kernels  10.4 us (22%)
  between operations  1.3 us (3%)
    all_to_all x3, blocking collectives, everywhere(): return lax.all_to_all(copies, ('row', 'col'), 0, 0, tiled=True)  35.6 us
    pallas_call x1, Pallas kernels, local(): pl.pallas_call(functools.partial(first_kernel, row_devices, col_devices,...  5.73 us
    pallas_call x1, Pallas kernels, local(): pl.pallas_call(functools.partial(second_kernel, col_devices, total_entrie...  2.14 us
    pallas_call x1, Pallas kernels, local(): pl.pallas_call(pack_kernel, out_shape=shaped(devices, 1, (LIST_ROW + 1) *...  1.69 us

profile of v2, /device:TPU:0, one launch (start us, length us, event | category | flops | bytes accessed | tf_op | source)
XLA Modules:
  0.0 47.3 jit_solution(1505420684501120105)
XLA Ops:
  1.3 1.7 %shard_map.59 = f32[32,1,1664]{2,1,0:T(1,128)} custom-call(f32[6,128]{1,0:T(8,128)} %refs_0_.1, f32[6,128]{1,0:T(8,128)} %refs_1_.1, s32[1,5,1,8]{3,2,1,0:T(1,128)} %bitcast.1, s32[1,1]{1,0:T(1,128)S(6)} %copy.6.refs_3_), custom_call_target="tpu_custom_call" | custom-call | tf_op jit(solution)/shard_map/pallas_call | solution.py:534
  3.0 16.7 %all_to_all.15.all_ref = f32[32,1,1664]{2,1,0:T(1,128)S(1)} all-to-all(f32[32,1,1664]{2,1,0:T(1,128)} %shard_map.59), channel_id=1, replica_groups=mesh['row'=4,'col'=8] {'row','col'}, dimensions={0} | all-to-all | bytes 425984 | tf_op jit(solution)/shard_map/all_to_all | solution.py:527
  19.7 5.7 %shard_map.60 = (f32[32,1,768]{2,1,0:T(1,128)S(1)}, s32[1557]{0:T(1024)S(1)}, f32[21120,128]{1,0:T(8,128)S(1)}, f32[2,128]{1,0:T(2,128)S(1)}) custom-call(f32[32,1,1664]{2,1,0:T(1,128)S(1)} %all_to_all.15.all_ref), custom_call_target="tpu_custom_call" | custom-call | tf_op jit(solution)/shard_map/pallas_call | solution.py:551
  25.4 10.1 %all_to_all.16.image_ref = f32[32,1,768]{2,1,0:T(1,128)S(1)} all-to-all(f32[32,1,768]{2,1,0:T(1,128)S(1)} %get-tuple-element.14), channel_id=1, replica_groups=mesh['row'=4,'col'=8] {'row','col'}, dimensions={0} | all-to-all | bytes 196608 | tf_op jit(solution)/shard_map/all_to_all | solution.py:527
  35.5 2.1 %shard_map.61 = (f32[32,1,128]{2,1,0:T(1,128)S(1)}, f32[2,8,128]{2,1,0:T(8,128)S(1)}, f32[1,128]{1,0:T(1,128)S(1)}) custom-call(s32[1557]{0:T(1024)S(1)} %get-tuple-element.11.item_ref, f32[21120,128]{1,0:T(8,128)S(1)} %get-tuple-element.12.coef_ref, f32[2,128]{1,0:T(2,128)S(1)} %get-tuple-element.13.kept_ref, f32[32,1,1664]{2,1,0:T(1,128)S(1)} %all_to_all.15.all_ref, ...), custom_call_target="tpu_custom_call" | custom-call | tf_op jit(solution)/shard_map/pallas_call | solution.py:571
  37.6 8.8 %all_to_all.17.line_ref = f32[32,1,128]{2,1,0:T(1,128)S(1)} all-to-all(f32[32,1,128]{2,1,0:T(1,128)S(1)} %get-tuple-element.17), channel_id=1, replica_groups=mesh['row'=4,'col'=8] {'row','col'}, dimensions={0} | all-to-all | bytes 32768 | tf_op jit(solution)/shard_map/all_to_all | solution.py:527
  46.5 0.8 %shard_map.62 = (f32[6,128]{1,0:T(8,128)}, f32[4]{0:T(128)}) custom-call(f32[2,8,128]{2,1,0:T(8,128)S(1)} %get-tuple-element.15.pair_ref, f32[1,128]{1,0:T(1,128)S(1)} %get-tuple-element.16.scalar_ref, f32[32,1,128]{2,1,0:T(1,128)S(1)} %all_to_all.17.line_ref), custom_call_target="tpu_custom_call" | custom-call | tf_op jit(solution)/shard_map/pallas_call | solution.py:583

commit v3 on v0

--- a/solution.py
+++ b/solution.py
@@ -22,7 +22,8 @@
 ITEM_MASK = 255
 LAYER = 16
 TESTS = 5
-GROUP = 4
+GROUP = 2
+UNROLL = 2
 TERMS = 20
 HELD = 128
 VMEM_LIMIT = 32 * 1024 * 1024
@@ -259,6 +260,15 @@
     return force + turn + [du_a]
 
 
+def several(body):
+    def step_of(step, totals):
+        for part in range(UNROLL):
+            totals = body(step * UNROLL + part, totals)
+        return totals
+
+    return step_of
+
+
 def group_items(step, item_ref, item_count):
     at = [step * GROUP + part for part in range(GROUP)]
     return [item_ref[1 + place] for place in at], [place >= item_count for place in at]
@@ -378,12 +388,12 @@
         return count
 
     items = lax.fori_loop(0, (entries + TESTS - 1) // TESTS, prepare, items)
-    for part in range(GROUP):
+    for part in range(GROUP * UNROLL):
         item_ref[1 + items + part] = own_code << ITEM_BITS
     item_ref[0] = items
 
-    held = coef_ref.shape[0] // (TERMS * GROUP * SUB)
-    steps = (items + GROUP - 1) // GROUP
+    held = coef_ref.shape[0] // (TERMS * GROUP * UNROLL * SUB)
+    steps = (items + GROUP * UNROLL - 1) // (GROUP * UNROLL)
     u = own_frame[3:]
     t = cross3(own_moved[3:], u)
     own_wide = [wide(line) for line in own_frame]
@@ -404,8 +414,8 @@
         return totals
 
     zero = jnp.zeros((SUB, member), jnp.float32)
-    totals = lax.fori_loop(0, jnp.minimum(steps, held), keep, (zero,) * 9)
-    totals = lax.fori_loop(held, steps, lambda step, before: derive(step, before)[1], totals)
+    totals = lax.fori_loop(0, jnp.minimum(steps, held), several(keep), (zero,) * 9)
+    totals = lax.fori_loop(held, steps, several(lambda step, before: derive(step, before)[1]), totals)
     sums = [folded(total) for total in totals]
     kept_ref[...] = jnp.concatenate(sums[7:], axis=0)
     spread(close(sums, sums[7], sums[8], u, t), out_ref)
@@ -449,8 +459,8 @@
 
     own_code = own * (1 << CODE_BITS) + 21
     items = item_ref[0]
-    held = coef_ref.shape[0] // (TERMS * GROUP * SUB)
-    steps = (items + GROUP - 1) // GROUP
+    held = coef_ref.shape[0] // (TERMS * GROUP * UNROLL * SUB)
+    steps = (items + GROUP * UNROLL - 1) // (GROUP * UNROLL)
 
     def moved_row(tile, k):
         return row_of(second_ref, tile, k, member)
@@ -476,8 +486,8 @@
         return added(totals, apply(partner_rows(moved_row, group, lanes), terms, own_wide, moved_wide))
 
     zero = jnp.zeros((SUB, member), jnp.float32)
-    totals = lax.fori_loop(0, jnp.minimum(steps, held), visit, (zero,) * 7)
-    totals = lax.fori_loop(held, steps, visit_again, totals)
+    totals = lax.fori_loop(0, jnp.minimum(steps, held), several(visit), (zero,) * 7)
+    totals = lax.fori_loop(held, steps, several(visit_again), totals)
     sums = [folded(total) for total in totals]
     product = close(sums, kept_ref[0:1, :], kept_ref[1:2, :], u, t)
     fill = [jnp.zeros((1, member), jnp.float32)] * (SUB - len(product))
@@ -554,7 +564,7 @@
         functools.partial(first_kernel, row_devices, col_devices, slots, period),
         out_shape=(
             shaped(devices, 1, dof * member),
-            jax.ShapeDtypeStruct((1 + longest * (member // SUB) + GROUP,), jnp.int32),
+            jax.ShapeDtypeStruct((1 + longest * (member // SUB) + GROUP * UNROLL,), jnp.int32),
             shaped(held_rows, member),
             shaped(2, member),
         ),

time: 46.6 us -> 48 us (1.030); the launches traced: 46.2 us -> 48.3 us
  blocking collectives: 35.8 us -> 38.5 us
  Pallas kernels: 9.13 us -> 8.52 us
    all_to_all x3, blocking collectives: 35.8 us -> 38.5 us  [everywhere(): return lax.all_to_all(copies, ('row', 'col'), 0, 0, tiled=True)]
where the time goes in v3:
time: 48 us; the launch traced here: 48.3 us
  blocking collectives  38.5 us (80%)
  Pallas kernels  8.52 us (18%)
  between operations  1.3 us (3%)
    all_to_all x3, blocking collectives, everywhere(): return lax.all_to_all(copies, ('row', 'col'), 0, 0, tiled=True)  38.5 us
    pallas_call x1, Pallas kernels, local(): pl.pallas_call(functools.partial(first_kernel, row_devices, col_devices,...  4.19 us
    pallas_call x1, Pallas kernels, local(): pl.pallas_call(functools.partial(second_kernel, col_devices, total_entrie...  1.83 us
    pallas_call x1, Pallas kernels, local(): pl.pallas_call(pack_kernel, out_shape=shaped(devices, 1, (LIST_ROW + 1) *...  1.69 us

profile of v3, /device:TPU:0, one launch (start us, length us, event | category | flops | bytes accessed | tf_op | source)
XLA Modules:
  0.0 48.3 jit_solution(3606168979238802499)
XLA Ops:
  1.3 1.7 %shard_map.59 = f32[32,1,1664]{2,1,0:T(1,128)} custom-call(f32[6,128]{1,0:T(8,128)} %refs_0_.1, f32[6,128]{1,0:T(8,128)} %refs_1_.1, s32[1,5,1,8]{3,2,1,0:T(1,128)} %bitcast.1, s32[1,1]{1,0:T(1,128)S(6)} %copy.6.refs_3_), custom_call_target="tpu_custom_call" | custom-call | tf_op jit(solution)/shard_map/pallas_call | solution.py:546
  3.0 16.7 %all_to_all.15.all_ref = f32[32,1,1664]{2,1,0:T(1,128)S(1)} all-to-all(f32[32,1,1664]{2,1,0:T(1,128)} %shard_map.59), channel_id=1, replica_groups=mesh['row'=4,'col'=8] {'row','col'}, dimensions={0} | all-to-all | bytes 425984 | tf_op jit(solution)/shard_map/all_to_all | solution.py:539
  19.7 4.2 %shard_map.60 = (f32[32,1,768]{2,1,0:T(1,128)S(1)}, s32[1557]{0:T(1024)S(1)}, f32[20480,128]{1,0:T(8,128)S(1)}, f32[2,128]{1,0:T(2,128)S(1)}) custom-call(f32[32,1,1664]{2,1,0:T(1,128)S(1)} %all_to_all.15.all_ref), custom_call_target="tpu_custom_call" | custom-call | tf_op jit(solution)/shard_map/pallas_call | solution.py:563
  23.9 12.8 %all_to_all.16.image_ref = f32[32,1,768]{2,1,0:T(1,128)S(1)} all-to-all(f32[32,1,768]{2,1,0:T(1,128)S(1)} %get-tuple-element.14), channel_id=1, replica_groups=mesh['row'=4,'col'=8] {'row','col'}, dimensions={0} | all-to-all | bytes 196608 | tf_op jit(solution)/shard_map/all_to_all | solution.py:539
  36.7 1.8 %shard_map.61 = (f32[32,1,128]{2,1,0:T(1,128)S(1)}, f32[2,8,128]{2,1,0:T(8,128)S(1)}, f32[1,128]{1,0:T(1,128)S(1)}) custom-call(s32[1557]{0:T(1024)S(1)} %get-tuple-element.11.item_ref, f32[20480,128]{1,0:T(8,128)S(1)} %get-tuple-element.12.coef_ref, f32[2,128]{1,0:T(2,128)S(1)} %get-tuple-element.13.kept_ref, f32[32,1,1664]{2,1,0:T(1,128)S(1)} %all_to_all.15.all_ref, ...), custom_call_target="tpu_custom_call" | custom-call | tf_op jit(solution)/shard_map/pallas_call | solution.py:583
  38.5 9.0 %all_to_all.17.line_ref = f32[32,1,128]{2,1,0:T(1,128)S(1)} all-to-all(f32[32,1,128]{2,1,0:T(1,128)S(1)} %get-tuple-element.17), channel_id=1, replica_groups=mesh['row'=4,'col'=8] {'row','col'}, dimensions={0} | all-to-all | bytes 32768 | tf_op jit(solution)/shard_map/all_to_all | solution.py:539
  47.5 0.8 %shard_map.62 = (f32[6,128]{1,0:T(8,128)}, f32[4]{0:T(128)}) custom-call(f32[2,8,128]{2,1,0:T(8,128)S(1)} %get-tuple-element.15.pair_ref, f32[1,128]{1,0:T(1,128)S(1)} %get-tuple-element.16.scalar_ref, f32[32,1,128]{2,1,0:T(1,128)S(1)} %all_to_all.17.line_ref), custom_call_target="tpu_custom_call" | custom-call | tf_op jit(solution)/shard_map/pallas_call | solution.py:595

commit v4 on v3

--- a/solution.py
+++ b/solution.py
@@ -22,8 +22,8 @@
 ITEM_MASK = 255
 LAYER = 16
 TESTS = 5
-GROUP = 2
-UNROLL = 2
+GROUP = 1
+UNROLL = 4
 TERMS = 20
 HELD = 128
 VMEM_LIMIT = 32 * 1024 * 1024

time: 48 us -> 46.4 us (0.967); the launches traced: 48.3 us -> 46.1 us
  blocking collectives: 38.5 us -> 36.3 us
    all_to_all x3, blocking collectives: 38.5 us -> 36.3 us  [everywhere(): return lax.all_to_all(copies, ('row', 'col'), 0, 0, tiled=True)]
where the time goes in v4:
time: 46.4 us; the launch traced here: 46.1 us
  blocking collectives  36.3 us (78%)
  Pallas kernels  8.51 us (18%)
  between operations  1.3 us (3%)
    all_to_all x3, blocking collectives, everywhere(): return lax.all_to_all(copies, ('row', 'col'), 0, 0, tiled=True)  36.3 us
    pallas_call x1, Pallas kernels, local(): pl.pallas_call(functools.partial(first_kernel, row_devices, col_devices,...  4.2 us
    pallas_call x1, Pallas kernels, local(): pl.pallas_call(functools.partial(second_kernel, col_devices, total_entrie...  1.82 us
    pallas_call x1, Pallas kernels, local(): pl.pallas_call(pack_kernel, out_shape=shaped(devices, 1, (LIST_ROW + 1) *...  1.69 us

profile of v4, /device:TPU:0, one launch (start us, length us, event | category | flops | bytes accessed | tf_op | source)
XLA Modules:
  0.0 46.1 jit_solution(13395020044797975527)
XLA Ops:
  1.3 1.7 %shard_map.59 = f32[32,1,1664]{2,1,0:T(1,128)} custom-call(f32[6,128]{1,0:T(8,128)} %refs_0_.1, f32[6,128]{1,0:T(8,128)} %refs_1_.1, s32[1,5,1,8]{3,2,1,0:T(1,128)} %bitcast.1, s32[1,1]{1,0:T(1,128)S(6)} %copy.6.refs_3_), custom_call_target="tpu_custom_call" | custom-call | tf_op jit(solution)/shard_map/pallas_call | solution.py:546
  3.0 16.7 %all_to_all.15.all_ref = f32[32,1,1664]{2,1,0:T(1,128)S(1)} all-to-all(f32[32,1,1664]{2,1,0:T(1,128)} %shard_map.59), channel_id=1, replica_groups=mesh['row'=4,'col'=8] {'row','col'}, dimensions={0} | all-to-all | bytes 425984 | tf_op jit(solution)/shard_map/all_to_all | solution.py:539
  19.7 4.2 %shard_map.60 = (f32[32,1,768]{2,1,0:T(1,128)S(1)}, s32[1557]{0:T(1024)S(1)}, f32[20480,128]{1,0:T(8,128)S(1)}, f32[2,128]{1,0:T(2,128)S(1)}) custom-call(f32[32,1,1664]{2,1,0:T(1,128)S(1)} %all_to_all.15.all_ref), custom_call_target="tpu_custom_call" | custom-call | tf_op jit(solution)/shard_map/pallas_call | solution.py:563
  23.9 10.7 %all_to_all.16.image_ref = f32[32,1,768]{2,1,0:T(1,128)S(1)} all-to-all(f32[32,1,768]{2,1,0:T(1,128)S(1)} %get-tuple-element.14), channel_id=1, replica_groups=mesh['row'=4,'col'=8] {'row','col'}, dimensions={0} | all-to-all | bytes 196608 | tf_op jit(solution)/shard_map/all_to_all | solution.py:539
  34.6 1.8 %shard_map.61 = (f32[32,1,128]{2,1,0:T(1,128)S(1)}, f32[2,8,128]{2,1,0:T(8,128)S(1)}, f32[1,128]{1,0:T(1,128)S(1)}) custom-call(s32[1557]{0:T(1024)S(1)} %get-tuple-element.11.item_ref, f32[20480,128]{1,0:T(8,128)S(1)} %get-tuple-element.12.coef_ref, f32[2,128]{1,0:T(2,128)S(1)} %get-tuple-element.13.kept_ref, f32[32,1,1664]{2,1,0:T(1,128)S(1)} %all_to_all.15.all_ref, ...), custom_call_target="tpu_custom_call" | custom-call | tf_op jit(solution)/shard_map/pallas_call | solution.py:583
  36.4 8.8 %all_to_all.17.line_ref = f32[32,1,128]{2,1,0:T(1,128)S(1)} all-to-all(f32[32,1,128]{2,1,0:T(1,128)S(1)} %get-tuple-element.17), channel_id=1, replica_groups=mesh['row'=4,'col'=8] {'row','col'}, dimensions={0} | all-to-all | bytes 32768 | tf_op jit(solution)/shard_map/all_to_all | solution.py:539
  45.3 0.8 %shard_map.62 = (f32[6,128]{1,0:T(8,128)}, f32[4]{0:T(128)}) custom-call(f32[2,8,128]{2,1,0:T(8,128)S(1)} %get-tuple-element.15.pair_ref, f32[1,128]{1,0:T(1,128)S(1)} %get-tuple-element.16.scalar_ref, f32[32,1,128]{2,1,0:T(1,128)S(1)} %all_to_all.17.line_ref), custom_call_target="tpu_custom_call" | custom-call | tf_op jit(solution)/shard_map/pallas_call | solution.py:595

commit v5 on v3

--- a/solution.py
+++ b/solution.py
@@ -23,7 +23,7 @@
 LAYER = 16
 TESTS = 5
 GROUP = 2
-UNROLL = 2
+UNROLL = 3
 TERMS = 20
 HELD = 128
 VMEM_LIMIT = 32 * 1024 * 1024

time: 48 us -> 47.1 us (0.981); the launches traced: 48.3 us -> 46.6 us
  blocking collectives: 38.5 us -> 37.4 us
  Pallas kernels: 8.52 us -> 7.84 us
    all_to_all x3, blocking collectives: 38.5 us -> 37.4 us  [everywhere(): return lax.all_to_all(copies, ('row', 'col'), 0, 0, tiled=True)]
where the time goes in v5:
time: 47.1 us; the launch traced here: 46.6 us
  blocking collectives  37.4 us (79%)
  Pallas kernels  7.84 us (17%)
  between operations  1.3 us (3%)
    all_to_all x3, blocking collectives, everywhere(): return lax.all_to_all(copies, ('row', 'col'), 0, 0, tiled=True)  37.4 us
    pallas_call x1, Pallas kernels, local(): pl.pallas_call(functools.partial(first_kernel, row_devices, col_devices,...  3.75 us
    pallas_call x1, Pallas kernels, local(): pl.pallas_call(pack_kernel, out_shape=shaped(devices, 1, (LIST_ROW + 1) *...  1.69 us
    pallas_call x1, Pallas kernels, local(): pl.pallas_call(functools.partial(second_kernel, col_devices, total_entrie...  1.6 us

profile of v5, /device:TPU:0, one launch (start us, length us, event | category | flops | bytes accessed | tf_op | source)
XLA Modules:
  0.0 46.6 jit_solution(3719293526691284897)
XLA Ops:
  1.3 1.7 %shard_map.59 = f32[32,1,1664]{2,1,0:T(1,128)} custom-call(f32[6,128]{1,0:T(8,128)} %refs_0_.1, f32[6,128]{1,0:T(8,128)} %refs_1_.1, s32[1,5,1,8]{3,2,1,0:T(1,128)} %bitcast.1, s32[1,1]{1,0:T(1,128)S(6)} %copy.6.refs_3_), custom_call_target="tpu_custom_call" | custom-call | tf_op jit(solution)/shard_map/pallas_call | solution.py:546
  3.0 16.7 %all_to_all.15.all_ref = f32[32,1,1664]{2,1,0:T(1,128)S(1)} all-to-all(f32[32,1,1664]{2,1,0:T(1,128)} %shard_map.59), channel_id=1, replica_groups=mesh['row'=4,'col'=8] {'row','col'}, dimensions={0} | all-to-all | bytes 425984 | tf_op jit(solution)/shard_map/all_to_all | solution.py:539
  19.7 3.8 %shard_map.60 = (f32[32,1,768]{2,1,0:T(1,128)S(1)}, s32[1559]{0:T(1024)S(1)}, f32[20480,128]{1,0:T(8,128)S(1)}, f32[2,128]{1,0:T(2,128)S(1)}) custom-call(f32[32,1,1664]{2,1,0:T(1,128)S(1)} %all_to_all.15.all_ref), custom_call_target="tpu_custom_call" | custom-call | tf_op jit(solution)/shard_map/pallas_call | solution.py:563
  23.4 11.8 %all_to_all.16.image_ref = f32[32,1,768]{2,1,0:T(1,128)S(1)} all-to-all(f32[32,1,768]{2,1,0:T(1,128)S(1)} %get-tuple-element.14), channel_id=1, replica_groups=mesh['row'=4,'col'=8] {'row','col'}, dimensions={0} | all-to-all | bytes 196608 | tf_op jit(solution)/shard_map/all_to_all | solution.py:539
  35.2 1.6 %shard_map.61 = (f32[32,1,128]{2,1,0:T(1,128)S(1)}, f32[2,8,128]{2,1,0:T(8,128)S(1)}, f32[1,128]{1,0:T(1,128)S(1)}) custom-call(s32[1559]{0:T(1024)S(1)} %get-tuple-element.11.item_ref, f32[20480,128]{1,0:T(8,128)S(1)} %get-tuple-element.12.coef_ref, f32[2,128]{1,0:T(2,128)S(1)} %get-tuple-element.13.kept_ref, f32[32,1,1664]{2,1,0:T(1,128)S(1)} %all_to_all.15.all_ref, ...), custom_call_target="tpu_custom_call" | custom-call | tf_op jit(solution)/shard_map/pallas_call | solution.py:583
  36.8 9.0 %all_to_all.17.line_ref = f32[32,1,128]{2,1,0:T(1,128)S(1)} all-to-all(f32[32,1,128]{2,1,0:T(1,128)S(1)} %get-tuple-element.17), channel_id=1, replica_groups=mesh['row'=4,'col'=8] {'row','col'}, dimensions={0} | all-to-all | bytes 32768 | tf_op jit(solution)/shard_map/all_to_all | solution.py:539
  45.8 0.8 %shard_map.62 = (f32[6,128]{1,0:T(8,128)}, f32[4]{0:T(128)}) custom-call(f32[2,8,128]{2,1,0:T(8,128)S(1)} %get-tuple-element.15.pair_ref, f32[1,128]{1,0:T(1,128)S(1)} %get-tuple-element.16.scalar_ref, f32[32,1,128]{2,1,0:T(1,128)S(1)} %all_to_all.17.line_ref), custom_call_target="tpu_custom_call" | custom-call | tf_op jit(solution)/shard_map/pallas_call | solution.py:595

commit v6 on v3

--- a/solution.py
+++ b/solution.py
@@ -21,7 +21,7 @@
 ITEM_BITS = 8
 ITEM_MASK = 255
 LAYER = 16
-TESTS = 5
+TESTS = 10
 GROUP = 2
 UNROLL = 2
 TERMS = 20

time: 48 us -> 46.3 us (0.965); the launches traced: 48.3 us -> 45.6 us
  blocking collectives: 38.5 us -> 36.1 us
    all_to_all x3, blocking collectives: 38.5 us -> 36.1 us  [everywhere(): return lax.all_to_all(copies, ('row', 'col'), 0, 0, tiled=True)]
where the time goes in v6:
time: 46.3 us; the launch traced here: 45.6 us
  blocking collectives  36.1 us (78%)
  Pallas kernels  8.23 us (18%)
  between operations  1.3 us (3%)
    all_to_all x3, blocking collectives, everywhere(): return lax.all_to_all(copies, ('row', 'col'), 0, 0, tiled=True)  36.1 us
    pallas_call x1, Pallas kernels, local(): pl.pallas_call(functools.partial(first_kernel, row_devices, col_devices,...  4.05 us
    pallas_call x1, Pallas kernels, local(): pl.pallas_call(pack_kernel, out_shape=shaped(devices, 1, (LIST_ROW + 1) *...  1.69 us
    pallas_call x1, Pallas kernels, local(): pl.pallas_call(functools.partial(second_kernel, col_devices, total_entrie...  1.68 us

profile of v6, /device:TPU:0, one launch (start us, length us, event | category | flops | bytes accessed | tf_op | source)
XLA Modules:
  0.0 45.6 jit_solution(10027700328179809319)
XLA Ops:
  1.3 1.7 %shard_map.59 = f32[32,1,1664]{2,1,0:T(1,128)} custom-call(f32[6,128]{1,0:T(8,128)} %refs_0_.1, f32[6,128]{1,0:T(8,128)} %refs_1_.1, s32[1,5,1,8]{3,2,1,0:T(1,128)} %bitcast.1, s32[1,1]{1,0:T(1,128)S(6)} %copy.6.refs_3_), custom_call_target="tpu_custom_call" | custom-call | tf_op jit(solution)/shard_map/pallas_call | solution.py:546
  3.0 16.7 %all_to_all.15.all_ref = f32[32,1,1664]{2,1,0:T(1,128)S(1)} all-to-all(f32[32,1,1664]{2,1,0:T(1,128)} %shard_map.59), channel_id=1, replica_groups=mesh['row'=4,'col'=8] {'row','col'}, dimensions={0} | all-to-all | bytes 425984 | tf_op jit(solution)/shard_map/all_to_all | solution.py:539
  19.7 4.1 %shard_map.60 = (f32[32,1,768]{2,1,0:T(1,128)S(1)}, s32[1557]{0:T(1024)S(1)}, f32[20480,128]{1,0:T(8,128)S(1)}, f32[2,128]{1,0:T(2,128)S(1)}) custom-call(f32[32,1,1664]{2,1,0:T(1,128)S(1)} %all_to_all.15.all_ref), custom_call_target="tpu_custom_call" | custom-call | tf_op jit(solution)/shard_map/pallas_call | solution.py:563
  23.7 10.5 %all_to_all.16.image_ref = f32[32,1,768]{2,1,0:T(1,128)S(1)} all-to-all(f32[32,1,768]{2,1,0:T(1,128)S(1)} %get-tuple-element.14), channel_id=1, replica_groups=mesh['row'=4,'col'=8] {'row','col'}, dimensions={0} | all-to-all | bytes 196608 | tf_op jit(solution)/shard_map/all_to_all | solution.py:539
  34.3 1.7 %shard_map.61 = (f32[32,1,128]{2,1,0:T(1,128)S(1)}, f32[2,8,128]{2,1,0:T(8,128)S(1)}, f32[1,128]{1,0:T(1,128)S(1)}) custom-call(s32[1557]{0:T(1024)S(1)} %get-tuple-element.11.item_ref, f32[20480,128]{1,0:T(8,128)S(1)} %get-tuple-element.12.coef_ref, f32[2,128]{1,0:T(2,128)S(1)} %get-tuple-element.13.kept_ref, f32[32,1,1664]{2,1,0:T(1,128)S(1)} %all_to_all.15.all_ref, ...), custom_call_target="tpu_custom_call" | custom-call | tf_op jit(solution)/shard_map/pallas_call | solution.py:583
  36.0 8.8 %all_to_all.17.line_ref = f32[32,1,128]{2,1,0:T(1,128)S(1)} all-to-all(f32[32,1,128]{2,1,0:T(1,128)S(1)} %get-tuple-element.17), channel_id=1, replica_groups=mesh['row'=4,'col'=8] {'row','col'}, dimensions={0} | all-to-all | bytes 32768 | tf_op jit(solution)/shard_map/all_to_all | solution.py:539
  44.8 0.8 %shard_map.62 = (f32[6,128]{1,0:T(8,128)}, f32[4]{0:T(128)}) custom-call(f32[2,8,128]{2,1,0:T(8,128)S(1)} %get-tuple-element.15.pair_ref, f32[1,128]{1,0:T(1,128)S(1)} %get-tuple-element.16.scalar_ref, f32[32,1,128]{2,1,0:T(1,128)S(1)} %all_to_all.17.line_ref), custom_call_target="tpu_custom_call" | custom-call | tf_op jit(solution)/shard_map/pallas_call | solution.py:595

commit v7 on v6

--- a/solution.py
+++ b/solution.py
@@ -23,7 +23,7 @@
 LAYER = 16
 TESTS = 10
 GROUP = 2
-UNROLL = 2
+UNROLL = 3
 TERMS = 20
 HELD = 128
 VMEM_LIMIT = 32 * 1024 * 1024

time: 46.3 us -> 46.5 us (level); the launches traced: 45.6 us -> 46.7 us
  blocking collectives: 36.1 us -> 37.3 us
    all_to_all x3, blocking collectives: 36.1 us -> 37.3 us  [everywhere(): return lax.all_to_all(copies, ('row', 'col'), 0, 0, tiled=True)]
where the time goes in v7:
time: 46.5 us; the launch traced here: 46.7 us
  blocking collectives  37.3 us (80%)
  Pallas kernels  8.04 us (17%)
  between operations  1.3 us (3%)
    all_to_all x3, blocking collectives, everywhere(): return lax.all_to_all(copies, ('row', 'col'), 0, 0, tiled=True)  37.3 us
    pallas_call x1, Pallas kernels, local(): pl.pallas_call(functools.partial(first_kernel, row_devices, col_devices,...  3.95 us
    pallas_call x1, Pallas kernels, local(): pl.pallas_call(pack_kernel, out_shape=shaped(devices, 1, (LIST_ROW + 1) *...  1.69 us
    pallas_call x1, Pallas kernels, local(): pl.pallas_call(functools.partial(second_kernel, col_devices, total_entrie...  1.6 us

profile of v7, /device:TPU:0, one launch (start us, length us, event | category | flops | bytes accessed | tf_op | source)
XLA Modules:
  0.0 46.7 jit_solution(3683651641361692394)
XLA Ops:
  1.3 1.7 %shard_map.59 = f32[32,1,1664]{2,1,0:T(1,128)} custom-call(f32[6,128]{1,0:T(8,128)} %refs_0_.1, f32[6,128]{1,0:T(8,128)} %refs_1_.1, s32[1,5,1,8]{3,2,1,0:T(1,128)} %bitcast.1, s32[1,1]{1,0:T(1,128)S(6)} %copy.6.refs_3_), custom_call_target="tpu_custom_call" | custom-call | tf_op jit(solution)/shard_map/pallas_call | solution.py:546
  3.0 16.7 %all_to_all.15.all_ref = f32[32,1,1664]{2,1,0:T(1,128)S(1)} all-to-all(f32[32,1,1664]{2,1,0:T(1,128)} %shard_map.59), channel_id=1, replica_groups=mesh['row'=4,'col'=8] {'row','col'}, dimensions={0} | all-to-all | bytes 425984 | tf_op jit(solution)/shard_map/all_to_all | solution.py:539
  19.7 4.0 %shard_map.60 = (f32[32,1,768]{2,1,0:T(1,128)S(1)}, s32[1559]{0:T(1024)S(1)}, f32[20480,128]{1,0:T(8,128)S(1)}, f32[2,128]{1,0:T(2,128)S(1)}) custom-call(f32[32,1,1664]{2,1,0:T(1,128)S(1)} %all_to_all.15.all_ref), custom_call_target="tpu_custom_call" | custom-call | tf_op jit(solution)/shard_map/pallas_call | solution.py:563
  23.6 11.6 %all_to_all.16.image_ref = f32[32,1,768]{2,1,0:T(1,128)S(1)} all-to-all(f32[32,1,768]{2,1,0:T(1,128)S(1)} %get-tuple-element.14), channel_id=1, replica_groups=mesh['row'=4,'col'=8] {'row','col'}, dimensions={0} | all-to-all | bytes 196608 | tf_op jit(solution)/shard_map/all_to_all | solution.py:539
  35.2 1.6 %shard_map.61 = (f32[32,1,128]{2,1,0:T(1,128)S(1)}, f32[2,8,128]{2,1,0:T(8,128)S(1)}, f32[1,128]{1,0:T(1,128)S(1)}) custom-call(s32[1559]{0:T(1024)S(1)} %get-tuple-element.11.item_ref, f32[20480,128]{1,0:T(8,128)S(1)} %get-tuple-element.12.coef_ref, f32[2,128]{1,0:T(2,128)S(1)} %get-tuple-element.13.kept_ref, f32[32,1,1664]{2,1,0:T(1,128)S(1)} %all_to_all.15.all_ref, ...), custom_call_target="tpu_custom_call" | custom-call | tf_op jit(solution)/shard_map/pallas_call | solution.py:583
  36.8 9.0 %all_to_all.17.line_ref = f32[32,1,128]{2,1,0:T(1,128)S(1)} all-to-all(f32[32,1,128]{2,1,0:T(1,128)S(1)} %get-tuple-element.17), channel_id=1, replica_groups=mesh['row'=4,'col'=8] {'row','col'}, dimensions={0} | all-to-all | bytes 32768 | tf_op jit(solution)/shard_map/all_to_all | solution.py:539
  45.9 0.8 %shard_map.62 = (f32[6,128]{1,0:T(8,128)}, f32[4]{0:T(128)}) custom-call(f32[2,8,128]{2,1,0:T(8,128)S(1)} %get-tuple-element.15.pair_ref, f32[1,128]{1,0:T(1,128)S(1)} %get-tuple-element.16.scalar_ref, f32[32,1,128]{2,1,0:T(1,128)S(1)} %all_to_all.17.line_ref), custom_call_target="tpu_custom_call" | custom-call | tf_op jit(solution)/shard_map/pallas_call | solution.py:595
